TPU v7x, 512 devices: a whole 4x8x8 slice. The times are simulated.
512 devices in a mesh: shot: 32 (over y, z_hi), point: 16 (over z_lo, x, core).
Axes of the slice: x: 4, y: 8, z: 8 (z_hi: 4, z_lo: 2; z = z_hi * 2 + z_lo), core: 2. Of those that a mesh axis runs over, the one named last changes fastest.
Arguments:
- traces: bfloat16 [64, 32, 1024], P('shot', 'point'), may hold values from -6 to 6
- panels: bfloat16 [32, 256, 1024], P('point', 'shot'), may hold values from -0.09375 to 0.09375
- aperture: int32 [64, 32], P('shot', 'point'), may hold values 0 or 1
- window_lo: int32 [256, 64], P('point', 'shot'), may hold values from 0 to 255
- window_hi: int32 [256, 64], P('point', 'shot'), may hold values from 512 to 1023
Outputs:
- multiples: bfloat16 [256, 64, 1024], P('point', 'shot')
All inputs are finite; a program needn't handle non-finite values. No bound on the sum of `aperture` on one device may be relied on, other than what follows from the above.
Results may differ from a plain program's by a relative error of at most 0.001.
Values may be sent and summed in bfloat16 or wider, within the bound.
A program may use at most 64 MiB of HBM per device.

v0:
```python
import jax
import jax.numpy as jnp
from jax import lax
from jax.sharding import PartitionSpec as P


def toeplitz(series):
    count = series.shape[-1]
    padded = jnp.concatenate([series, jnp.zeros_like(series)], -1)
    tiled_flat = jnp.tile(padded, (1, count))[:, : count * (2 * count - 1)]
    return tiled_flat.reshape(series.shape[0], count, 2 * count - 1)[:, :, :count]


def window_weights(window_lo, window_hi, length):
    sample_axis = jnp.arange(length).astype(jnp.float32)[None, None, :]
    lower = window_lo.astype(jnp.float32)[:, :, None]
    upper = window_hi.astype(jnp.float32)[:, :, None]
    rising = jnp.clip((sample_axis - lower + 32.0) / 32.0, 0.0, 1.0)
    falling = jnp.clip((upper - sample_axis) / 32.0, 0.0, 1.0)
    return rising * falling


def body(traces, panels, aperture, window_lo, window_hi):
    masked = traces * aperture[:, :, None].astype(traces.dtype)
    local_points = masked.shape[1]

    def kernel_maker():

        def kernel_for(point):
            return toeplitz(lax.dynamic_index_in_dim(masked, point, 1, keepdims=False))

        return kernel_for

    def make_convolve(kernel_for):

        def convolve(panel_piece, first_row):

            def one_point(point, total_sum):
                panel_rows = lax.dynamic_index_in_dim(panel_piece, point, 0, keepdims=False)
                return total_sum + jnp.einsum(
                    "ru,sut->rst", panel_rows, kernel_for(point), preferred_element_type=jnp.float32
                )

            initial = jnp.zeros(
                (panel_piece.shape[1], masked.shape[0], masked.shape[2]), jnp.float32
            )
            return lax.fori_loop(0, local_points, one_point, initial)

        return convolve

    convolve = make_convolve(kernel_maker())
    partial_terms = convolve(lax.all_gather(panels, "shot", axis=1, tiled=True), jnp.int32(0))
    predicted = lax.psum_scatter(partial_terms, "point", scatter_dimension=0, tiled=True)
    weights = window_weights(window_lo, window_hi, traces.shape[2])
    return (weights * predicted).astype(jnp.bfloat16)


def solution(mesh):
    in_specs = (
        P("shot", "point", None),
        P("point", "shot", None),
        P("shot", "point"),
        P("point", "shot"),
        P("point", "shot"),
    )
    out_specs = P("point", "shot", None)
    return jax.shard_map(body, mesh=mesh, in_specs=in_specs, out_specs=out_specs, check_vma=False)
```

profile of v0, /device:TPU:1, one launch (start us, length us, event | category | flops | bytes accessed | tf_op | source)
XLA Modules:
  0.0 359.0 jit_solution(9905600033228501757)
XLA Ops:
  6.5 0.0 all-gather.2.cloned.1.call-start
  6.5 0.7 all-gather.2.cloned.1.call-update
  7.3 0.0 all-reduce.4.cloned.1.call-start
  7.3 0.7 convert_element_type.25
  8.0 0.1 copy.18
  8.1 0.8 copy_multiply_fusion
  8.9 87.5 %all-gather.2.cloned.1.call-done = bf16[2,256,1024]{2,1,0:T(8,128)(2,1)} async-done(((bf16[2,8,1024]{2,1,0:T(8,128)(2,1)}), bf16[2,256,1024]{2,1,0:T(8,128)(2,1)}) %all-gather.2.cloned.1.call-update) | async-done | bytes 1048592 | tf_op jit(solution)/shard_map/all_gather | solution.py:52
  96.4 117.5 %while.14 = (s32[]{:T(128)}, f32[256,2,1024]{2,0,1:T(8,128)S(1)}, bf16[2,256,1024]{2,1,0:T(8,128)(2,1)}, bf16[2,2,1024]{2,0,1:T(2,128)(2,1)S(1)}, s32[]{:T(128)}, /*index=5*/bf16[]{:T(256)}, s32[]{:T(128)}) while((s32[]{:T(128)}, f32[256,2,1024]{2,0,1:T(8,128)S(1)}, bf16[2,256,1024]{2,1,0:T(8,128)(2,1)}, ...), condition=%wide.region_1.2_spmd.clone, body=%wide.region_0.1_spmd.clone.sunk | while | flops 1074790400 | bytes 88609400 | solution.py:47
  96.4 1.1 broadcast_bitcast_fusion.2
  97.4 17.3 %copy.24 = bf16[1,2,1024,2048]{3,1,2,0:T(2,128)(2,1)S(1)} copy(bf16[1,2,1024,2048]{3,2,1,0:T(8,128)(2,1)S(1)} %broadcast_bitcast_fusion.2) | data formatting | bytes 16777216 | tf_op jit(solution)/shard_map/while
  114.8 7.2 %slice.25 = bf16[2,2096128]{1,0:T(2,128)(2,1)} slice(bf16[2,2097152]{1,0:T(2,128)(2,1)S(1)} %bitcast.18), slice={[0:2], [0:2096128]} | slice | bytes 16769024 | tf_op jit(solution)/shard_map/while/body/eval_jaxpr/slice | solution.py:10
  121.9 11.9 %reshape.26 = bf16[4192256]{0:T(1024)(128)(2,1)} reshape(bf16[2,2096128]{1,0:T(2,128)(2,1)} %slice.25) | data formatting | bytes 16769024 | tf_op jit(solution)/shard_map/while
  133.8 0.0 copy-start.2
  133.8 17.4 %reshape.27 = bf16[2,1024,2047]{2,1,0:T(8,128)(2,1)} reshape(bf16[4192256]{0:T(1024)(128)(2,1)} %reshape.26) | data formatting | bytes 16769024 | tf_op jit(solution)/shard_map/while/body/eval_jaxpr/reshape | solution.py:11
  151.2 0.0 copy-done.2
  151.2 3.9 %select_add_fusion.2 = f32[256,2,1024]{2,0,1:T(8,128)S(1)} fusion(f32[256,2,1024]{2,0,1:T(8,128)S(1)} %get-tuple-element.141, bf16[2,1024,2047]{2,1,0:T(8,128)(2,1)} %reshape.27, pred[]{:T(512)S(6)} %compare.4, bf16[2,256,1024]{2,1,0:T(8,128)(2,1)S(1)} %copy-done.2, s32[]{:T(128)} %get-tuple-element.140), kind=kOutput, calls=%fused_computation.3.clone.1 | convolution fusion | flops 1074790400 | bytes 8913409 | tf_op jit(solution)/shard_map/while/body/eval_jaxpr/ru,sut->rst/dot_general | solution.py:40
  155.2 1.1 broadcast_bitcast_fusion.2
  156.2 17.3 %copy.24 = bf16[1,2,1024,2048]{3,1,2,0:T(2,128)(2,1)S(1)} copy(bf16[1,2,1024,2048]{3,2,1,0:T(8,128)(2,1)S(1)} %broadcast_bitcast_fusion.2) | data formatting | bytes 16777216 | tf_op jit(solution)/shard_map/while
  173.6 7.2 %slice.25 = bf16[2,2096128]{1,0:T(2,128)(2,1)} slice(bf16[2,2097152]{1,0:T(2,128)(2,1)S(1)} %bitcast.18), slice={[0:2], [0:2096128]} | slice | bytes 16769024 | tf_op jit(solution)/shard_map/while/body/eval_jaxpr/slice | solution.py:10
  180.7 11.9 %reshape.26 = bf16[4192256]{0:T(1024)(128)(2,1)} reshape(bf16[2,2096128]{1,0:T(2,128)(2,1)} %slice.25) | data formatting | bytes 16769024 | tf_op jit(solution)/shard_map/while
  192.6 17.4 %reshape.27 = bf16[2,1024,2047]{2,1,0:T(8,128)(2,1)} reshape(bf16[4192256]{0:T(1024)(128)(2,1)} %reshape.26) | data formatting | bytes 16769024 | tf_op jit(solution)/shard_map/while/body/eval_jaxpr/reshape | solution.py:11
  210.0 0.0 copy-done.2
  210.0 3.9 %select_add_fusion.2 = f32[256,2,1024]{2,0,1:T(8,128)S(1)} fusion(f32[256,2,1024]{2,0,1:T(8,128)S(1)} %get-tuple-element.141, bf16[2,1024,2047]{2,1,0:T(8,128)(2,1)} %reshape.27, pred[]{:T(512)S(6)} %compare.4, bf16[2,256,1024]{2,1,0:T(8,128)(2,1)S(1)} %copy-done.2, s32[]{:T(128)} %get-tuple-element.140), kind=kOutput, calls=%fused_computation.3.clone.1 | convolution fusion | flops 1074790400 | bytes 8913409 | tf_op jit(solution)/shard_map/while/body/eval_jaxpr/ru,sut->rst/dot_general | solution.py:40
  213.9 2.9 copy.20
  216.8 0.0 all-reduce.4.cloned.1.call-update
  216.9 0.6 copy-done
  217.5 0.1 copy.16
  217.6 0.0 copy-done.1
  217.6 0.1 copy.17
  217.7 1.3 dynamic-slice
  219.6 130.8 %all-reduce.4.cloned.1.call-done = f32[256,2,1024]{2,1,0:T(2,128)} async-done(((f32[256,2,1024]{2,1,0:T(2,128)}), f32[256,2,1024]{2,1,0:T(2,128)}) %all-reduce.4.cloned.1.call-update) | async-done | bytes 2097168
  350.4 1.8 fusion.7
  (11 shorter events, 0.1 us)
Async XLA Ops:
  6.5 89.8 %all-gather.2.cloned.1.call-start = ((), (), s32[]{:S(2)}) async-start(), calls=%async_computation | async-start | bytes 1081344 | tf_op jit(solution)/shard_map/all_gather | solution.py:52
  7.3 343.1 %all-reduce.4.cloned.1.call-start = ((), (), s32[]{:S(2)}) async-start(), calls=%async_computation.1 | async-start | bytes 4194304
  133.8 17.4 %copy-start.2 = (bf16[2,256,1024]{2,1,0:T(8,128)(2,1)S(1)}, bf16[2,256,1024]{2,1,0:T(8,128)(2,1)}, u32[]{:S(2)}) copy-start(bf16[2,256,1024]{2,1,0:T(8,128)(2,1)} %get-tuple-element.149) | copy-start | bytes 3145732 | tf_op jit(solution)/shard_map/while
  192.6 17.4 %copy-start.2 = (bf16[2,256,1024]{2,1,0:T(8,128)(2,1)S(1)}, bf16[2,256,1024]{2,1,0:T(8,128)(2,1)}, u32[]{:S(2)}) copy-start(bf16[2,256,1024]{2,1,0:T(8,128)(2,1)} %get-tuple-element.149) | copy-start | bytes 3145732 | tf_op jit(solution)/shard_map/while
  216.8 0.7 copy-start
  216.8 0.8 copy-start.1
Sparse Core Ops, SparseCore 0:
  10.5 85.7 all-gather.1
  217.0 133.3 all-reduce.3
where the time goes:
time: 359 us
  waiting for transfers between devices  219 us (61%)
  local copies, waits for them, and re-layouts  115 us (32%)
  between operations  14.1 us (4%)
  matrix products  7.74 us (2%)
    unnamed x3, waiting for transfers between devices  131 us
    all_gather x1, waiting for transfers between devices, body(): lax.all_gather(panels, 'shot', axis=1, tiled=True)  87.5 us
    while x10, local copies, waits for them, and re-layouts  60.6 us
    reshape x2, local copies, waits for them, and re-layouts, toeplitz(): tiled_flat.reshape(series.shape[0], count, 2 * count - 1)[:, :, :count]  34.8 us
    slice x2, local copies, waits for them, and re-layouts, toeplitz(): tiled_flat = jnp.tile(padded, (1, count))[:, :count * (2 * count - 1)]  14.3 us
    dot_general x2, matrix products, one_point(): jnp.einsum('ru,sut->rst', panel_rows, kernel_for(point), preferred_elemen...  7.74 us
  transfers between devices with their start and end apart: 2, of which 2 were waited for; matrix products, arithmetic and copies ran while one was open for 1% of the time, Pallas kernels for 0%

commit v1 on v0

v1 whole, which is shorter than its diff:
```python
import jax
import jax.numpy as jnp
from jax import lax
from jax.experimental import pallas as pl
from jax.experimental.pallas import tpu as pltpu
from jax.sharding import PartitionSpec as P

F32, BF16 = jnp.float32, jnp.bfloat16
MESH = pl.DeviceIdType.MESH


def device(y, zh, zl, x, core):
    return (y * 4 + zh, (zl * 4 + x) * 2 + core)


def lane_index(rows):
    return lax.broadcasted_iota(jnp.int32, (rows, 128), 1)


def spread_panels(panel_in, left, g):
    for first in (0, 4):
        blocks = [
            [panel_in[g, b, :, q * 128 : (q + 1) * 128].astype(F32) for b in range(8)]
            for q in range(first, first + 4)
        ]
        rows = [jnp.concatenate([b[p][:8] for b in blocks], 0) for p in range(8)]
        rows += [jnp.concatenate([b[p][8:] for b in blocks], 0) for p in range(8)]
        lane = lane_index(32)
        for bit in (1, 2, 4, 8):
            low = (lane & bit) == 0
            new = list(rows)
            for p in range(16):
                if not p & bit:
                    lo, hi = rows[p], rows[p | bit]
                    new[p] = jnp.where(low, lo, pltpu.roll(hi, bit, 1))
                    new[p | bit] = jnp.where(low, pltpu.roll(lo, 128 - bit, 1), hi)
            rows = new
        for i in range(4):
            q = first + i
            at = ((q // 2) * 4 + g * 2 + q % 2) * 128
            left[:, at : at + 128] = jnp.concatenate([v[8 * i : 8 * i + 8] for v in rows], 0).astype(BF16)


def shift_traces(wide, right, slot, s):
    lane = lane_index(16)

    def one(g, carry):
        base = g * 256 + s * 16
        tiles = [
            jnp.concatenate([wide[pl.ds(base + p * 8 + q, 8, stride=32), :] for p in range(2)], 0)
            for q in range(8)
        ]
        for m in range(8):
            turned = [pltpu.roll(v, 16 * m, 1) if m else v for v in tiles]
            for q in range(8):
                value = turned[q]
                if m:
                    value = jnp.where(lane < 16 * m, turned[q - 1] if q else 0.0, value)
                value = value.astype(BF16)
                for h in range(2):
                    k = q + h
                    if k < 8:
                        row = pl.multiple_of((3 - k // 2) * 512 + g * 256 + h * 128 + m * 16, 16)
                        right[slot, pl.ds(row, 16), (k % 2) * 128 : (k % 2) * 128 + 128] = value
        return carry

    lax.fori_loop(0, 2, one, 0)


def convolve(left, right, slot):
    tiles = []
    for n in range(4):
        z = jnp.dot(
            left[:, : (n + 1) * 512], right[slot, (3 - n) * 512 :, :], preferred_element_type=F32
        )
        tiles += [z[:, :128], z[:, 128:]]
    for k in (8, 4, 2, 1):
        lane = lane_index(8 * k)
        turned = [pltpu.roll(z[k * 8 :], k, 1) for z in tiles]
        tiles = [
            z[: k * 8] + jnp.where(lane < k, turned[q - 1] if q else 0.0, turned[q])
            for q, z in enumerate(tiles)
        ]
    return tiles


def weigh(tiles, lower, upper):
    out = []
    for q, z in enumerate(tiles):
        t = (lane_index(8) + 128 * q).astype(F32)
        rising = jnp.clip((t - lower + 32.0) / 32.0, 0.0, 1.0)
        falling = jnp.clip((upper - t) / 32.0, 0.0, 1.0)
        out.append(rising * falling * z)
    return jnp.concatenate(out, 1)


def kernel(
    panels, traces, aperture, lo, hi, out,
    trace_raw, aperture_raw, lo_raw, hi_raw, trace_wide, trace_out, window_out,
    panel_in, trace_in, window_in, wide, left, right, result_out,
    local_sem, panel_send, panel_recv, pass_send, pass_recv,
    trace_send, trace_recv, window_send, window_recv, result_send, result_recv,
):
    shot, point = lax.axis_index("shot"), lax.axis_index("point")
    y, zh = shot // 4, shot % 4
    zl, x, core = point // 8, (point // 2) % 4, point % 2
    z = zh * 2 + zl
    half = zh // 2
    place = zl * 4 + x

    def start(source, target, send, recv, to):
        pltpu.make_async_remote_copy(
            src_ref=source, dst_ref=target, send_sem=send, recv_sem=recv, device_id=to, device_id_type=MESH
        ).start()

    def landed(ref, sem):
        pltpu.make_async_copy(ref, ref, sem).wait()

    loads = [
        pltpu.make_async_copy(source, target, local_sem.at[i])
        for i, (source, target) in enumerate(
            [(traces, trace_raw), (aperture, aperture_raw), (lo, lo_raw), (hi, hi_raw)]
        )
    ]
    for load in loads:
        load.start()

    barrier = pltpu.get_barrier_semaphore()

    def greet(to):
        pl.semaphore_signal(barrier, inc=1, device_id=to, device_id_type=MESH)

    def greet_traces(i, carry):
        greet(device(y, core * 2 + i // 16, (i // 8) % 2, (i // 2) % 4, i % 2))
        return carry

    def greet_panels(i, carry):
        greet(device(place, zh, i // 4, i % 4, core))
        return carry

    lax.fori_loop(0, 32, greet_traces, 0)
    lax.fori_loop(0, 8, greet_panels, 0)
    for i in range(2):
        greet(device(y, core * 2 + i, zl, x, half))
    greet(device(y, zh, zl, x, 1 - core))

    for load in loads:
        load.wait()
    for s in range(2):
        row = trace_raw[s].astype(F32)
        for p in range(2):
            kept = row[p : p + 1, :] * aperture_raw[s : s + 1, p : p + 1].astype(F32)
            for q in range(8):
                trace_wide[s * 16 + p * 8 + q : s * 16 + p * 8 + q + 1, :] = kept[:, q * 128 : (q + 1) * 128]
    trace_out[...] = trace_wide[...].astype(BF16)
    window_out[:, 0:2] = lo_raw[...].astype(F32)
    window_out[:, 2:4] = hi_raw[...].astype(F32)
    for slot in range(4):
        for g in range(2):
            right[slot, 1536 + g * 256 + 128 : 1536 + g * 256 + 256, 0:128] = jnp.zeros((128, 128), BF16)

    pl.semaphore_wait(barrier, 43)

    mine = (y // 4 == zl) & (y % 4 == x)

    def send_panel(i, carry):
        k = 4 + ((i + 1) // 2) * (2 * ((i + 1) % 2) - 1)
        start(
            panels, panel_in.at[0, place], panel_send, panel_recv.at[place],
            device((y + k) % 8, zh, y // 4, y % 4, core),
        )
        return carry

    lax.fori_loop(0, 7, send_panel, 0)

    @pl.when(mine)
    def _():
        pltpu.make_async_copy(panels, panel_in.at[0, place], panel_recv.at[place]).start()

    @pl.when(jnp.logical_not(mine))
    def _():
        start(
            panels, panel_in.at[0, place], panel_send, panel_recv.at[place], device(y, zh, y // 4, y % 4, core)
        )

    trace_slot = (zh % 2) * 16 + ((core + half) % 2) * 8 + place
    trace_sem = trace_recv.at[zh % 2]
    trace_target = trace_in.at[trace_slot]

    def send_trace(i, carry):
        o = i // 4
        dz = 4 + ((o + 1) // 2) * (2 * ((o + 1) % 2) - 1)
        to = (z + dz) % 8
        start(
            trace_out, trace_target, trace_send, trace_sem, device(y, to // 2, to % 2, (x + 3 - i % 4) % 4, half)
        )
        return carry

    lax.fori_loop(0, 31, send_trace, 0)

    @pl.when(core == half)
    def _():
        pltpu.make_async_copy(trace_out, trace_target, trace_sem).start()

    @pl.when(core != half)
    def _():
        start(trace_out, trace_target, trace_send, trace_sem, device(y, zh, zl, x, half))

    for i in range(2):
        rows = window_out.at[pl.ds(i * 8, 8)]
        to = core * 2 + i
        same = (core == half) & (zh % 2 == i)
        target, sem = window_in.at[zh % 2], window_recv.at[zh % 2]

        @pl.when(same)
        def _():
            pltpu.make_async_copy(rows, target, sem).start()

        @pl.when(jnp.logical_not(same))
        def _():
            start(rows, target, window_send.at[i], sem, device(y, to, zl, x, half))

    for b in range(8):
        landed(panel_in.at[0, b], panel_recv.at[b])
        start(
            panel_in.at[0, b], panel_in.at[1, b], pass_send, pass_recv, device(y, zh, zl, x, 1 - core)
        )
    spread_panels(panel_in, left, 0)
    for part in range(2):
        landed(trace_in.at[pl.ds(part * 16, 16)], trace_recv.at[part])
        wide[...] = trace_in[part * 16 : part * 16 + 16].reshape(512, 128).astype(F32)
        for s in range(2):
            shift_traces(wide, right, part * 2 + s, s)
    landed(panel_in.at[1], pass_recv)
    spread_panels(panel_in, left, 1)
    for part in range(2):
        landed(window_in.at[part], window_recv.at[part])
        for s in range(2):
            value = weigh(
                convolve(left, right, part * 2 + s),
                window_in[part, :, s : s + 1],
                window_in[part, :, 2 + s : 3 + s],
            )
            wide_rows = value.astype(BF16)
            result_out[part, s * 8 : s * 8 + 8, :] = wide_rows
        same = (core == half) & (zh % 2 == part)
        target, sem = out.at[zh % 2], result_recv.at[zh % 2]

        @pl.when(same)
        def _():
            pltpu.make_async_copy(result_out.at[part], target, sem).start()

        @pl.when(jnp.logical_not(same))
        def _():
            start(
                result_out.at[part], target, result_send.at[part], sem, device(y, core * 2 + part, zl, x, half)
            )

    for part in range(2):
        landed(out.at[part], result_recv.at[part])

    @pl.when(mine)
    def _():
        landed(panel_in.at[0, pl.ds(0, 7)], panel_send)

    @pl.when(jnp.logical_not(mine))
    def _():
        landed(panel_in.at[0], panel_send)

    @pl.when(core == half)
    def _():
        landed(trace_in.at[pl.ds(0, 31)], trace_send)

    @pl.when(core != half)
    def _():
        landed(trace_in, trace_send)

    landed(panel_in.at[1], pass_send)
    for i in range(2):
        same = (core == half) & (zh % 2 == i)

        @pl.when(jnp.logical_not(same))
        def _():
            landed(window_in.at[i], window_send.at[i])
            landed(result_out.at[i], result_send.at[i])


def body(traces, panels, aperture, window_lo, window_hi):
    anywhere = pl.BlockSpec(memory_space=pl.ANY)
    out = pl.pallas_call(
        kernel,
        out_shape=jax.ShapeDtypeStruct((2, 16, 1024), BF16),
        in_specs=[anywhere] * 5,
        out_specs=pl.BlockSpec(memory_space=pltpu.VMEM),
        scratch_shapes=[
            pltpu.VMEM((2, 2, 1024), BF16),
            pltpu.VMEM((2, 2), jnp.int32),
            pltpu.VMEM((16, 2), jnp.int32),
            pltpu.VMEM((16, 2), jnp.int32),
            pltpu.VMEM((32, 128), F32),
            pltpu.VMEM((32, 128), BF16),
            pltpu.VMEM((16, 128), F32),
            pltpu.VMEM((2, 8, 16, 1024), BF16),
            pltpu.VMEM((32, 32, 128), BF16),
            pltpu.VMEM((2, 8, 128), F32),
            pltpu.VMEM((512, 128), F32),
            pltpu.VMEM((128, 2048), BF16),
            pltpu.VMEM((4, 2048, 256), BF16),
            pltpu.VMEM((2, 16, 1024), BF16),
            pltpu.SemaphoreType.DMA((4,)),
            pltpu.SemaphoreType.DMA,
            pltpu.SemaphoreType.DMA((8,)),
            pltpu.SemaphoreType.DMA,
            pltpu.SemaphoreType.DMA,
            pltpu.SemaphoreType.DMA,
            pltpu.SemaphoreType.DMA((2,)),
            pltpu.SemaphoreType.DMA((2,)),
            pltpu.SemaphoreType.DMA((2,)),
            pltpu.SemaphoreType.DMA((2,)),
            pltpu.SemaphoreType.DMA((2,)),
        ],
        compiler_params=pltpu.CompilerParams(
            collective_id=0, has_side_effects=True, vmem_limit_bytes=40 << 20
        ),
    )(panels.reshape(16, 1024), traces, aperture, window_lo, window_hi)
    return out.reshape(2, 2, 8, 1024).transpose(0, 2, 1, 3).reshape(16, 2, 1024)


def solution(mesh):
    in_specs = (
        P("shot", "point", None),
        P("point", "shot", None),
        P("shot", "point"),
        P("point", "shot"),
        P("point", "shot"),
    )
    out_specs = P("point", "shot", None)
    return jax.shard_map(body, mesh=mesh, in_specs=in_specs, out_specs=out_specs, check_vma=False)
```

time: 359 us -> 37.5 us (0.10)
  waiting for transfers between devices: 219 us -> 0 us
  local copies, waits for them, and re-layouts: 115 us -> 3.49 us
  Pallas kernels: 0 us -> 33.7 us
  between operations: 14.1 us -> 0.02 us
  matrix products: 7.74 us -> 0 us
    unnamed x3 -> x0, waiting for transfers between devices: 131 us -> none
    all_gather x1 -> x0, waiting for transfers between devices: 87.5 us -> none  [body(): lax.all_gather(panels, 'shot', axis=1, tiled=True)]
    while x11 -> x0, local copies, waits for them, and re-layouts: 63.5 us -> none
    reshape x2 -> x0, local copies, waits for them, and re-layouts: 34.8 us -> none  [toeplitz(): tiled_flat.reshape(series.shape[0], count, 2 * count - 1)[:, :, :count]]
    pallas_call x0 -> x1, Pallas kernels: none -> 33.7 us  [body(): pl.pallas_call(kernel, out_shape=jax.ShapeDtypeStruct((2, 16, 1024), BF16...]
    slice x2 -> x0, local copies, waits for them, and re-layouts: 14.3 us -> none  [toeplitz(): tiled_flat = jnp.tile(padded, (1, count))[:, :count * (2 * count - 1)]]
    dot_general x2 -> x0, matrix products: 7.74 us -> none  [one_point(): jnp.einsum('ru,sut->rst', panel_rows, kernel_for(point), preferred_elemen...]
  transfers between devices with their start and end apart: 2 -> 0, of which waited for: 2 -> 0; matrix products, arithmetic and copies ran while one was open for 1% -> 0% of each run, Pallas kernels for 0% -> 0%
where the time goes in v1:
time: 37.5 us; the launch traced here: 37.2 us
  Pallas kernels  33.7 us (90%)
  local copies, waits for them, and re-layouts  3.49 us (9%)
    pallas_call x1, Pallas kernels, body(): pl.pallas_call(kernel, out_shape=jax.ShapeDtypeStruct((2, 16, 1024), BF16...  33.7 us
    unnamed x12, local copies, waits for them, and re-layouts  2.79 us

profile of v1, /device:TPU:1, one launch (start us, length us, event | category | flops | bytes accessed | tf_op | source)
XLA Modules:
  0.0 37.2 jit_solution(771668333106573362)
XLA Ops:
  0.0 0.0 copy-start.3
  0.0 0.7 %copy-done.3 = s32[16,2]{0,1:T(2,128)S(1)} copy-done((s32[16,2]{0,1:T(2,128)S(1)}, s32[16,2]{0,1:T(2,128)}, u32[]{:S(2)}) %copy-start.3) | copy-done | bytes 152
  0.7 0.0 copy-start.4
  0.7 0.0 copy-start.1
  0.7 0.1 copy.6.lo
  0.8 0.6 %copy-done.4 = s32[16,2]{0,1:T(2,128)S(1)} copy-done((s32[16,2]{0,1:T(2,128)S(1)}, s32[16,2]{0,1:T(2,128)}, u32[]{:S(2)}) %copy-start.4) | copy-done | bytes 152
  1.4 0.0 copy-start.2
  1.4 0.1 copy.7.hi
  1.4 0.0 copy-done.1
  1.4 0.6 %copy-done.2 = s32[2,2]{1,0:T(2,128)S(1)} copy-done((s32[2,2]{1,0:T(2,128)S(1)}, s32[2,2]{1,0:T(2,128)}, u32[]{:S(2)}) %copy-start.2) | copy-done | bytes 40
  2.0 0.0 copy-start
  2.0 0.8 %copy-done = bf16[2,8,1024]{2,1,0:T(8,128)(2,1)S(1)} copy-done((bf16[2,8,1024]{2,1,0:T(8,128)(2,1)S(1)}, bf16[2,8,1024]{2,1,0:T(8,128)(2,1)}, u32[]{:S(2)}) %copy-start) | copy-done | bytes 32792
  2.8 33.7 %shard_map.55 = bf16[2,16,1024]{2,1,0:T(8,128)(2,1)S(1)} custom-call(bf16[16,1024]{1,0:T(8,128)(2,1)S(1)} %bitcast.6, bf16[2,2,1024]{2,1,0:T(2,128)(2,1)S(1)} %copy-done.1, s32[2,2]{1,0:T(2,128)S(1)} %copy-done.2, s32[16,2]{1,0:T(8,128)S(1)} %copy.6.lo, s32[16,2]{1,0:T(8,128)S(1)} %copy.7.hi), custom_call_target="tpu_custom_call" | custom-call | tf_op jit(solution)/shard_map/pallas_call | solution.py:290
  36.5 0.7 %copy.8 = bf16[2,8,2,1024]{3,2,1,0:T(2,128)(2,1)} copy(bf16[2,8,2,1024]{3,1,2,0:T(8,128)(2,1)S(1)} %bitcast.5) | data formatting | bytes 131072 | tf_op jit(solution)/shard_map/transpose | solution.py:326
Async XLA Ops:
  0.0 0.7 %copy-start.3 = (s32[16,2]{0,1:T(2,128)S(1)}, s32[16,2]{0,1:T(2,128)}, u32[]{:S(2)}) copy-start(s32[16,2]{0,1:T(2,128)} %param.8) | copy-start | bytes 388
  0.7 0.7 %copy-start.4 = (s32[16,2]{0,1:T(2,128)S(1)}, s32[16,2]{0,1:T(2,128)}, u32[]{:S(2)}) copy-start(s32[16,2]{0,1:T(2,128)} %param.9) | copy-start | bytes 388
  0.7 0.8 %copy-start.1 = (bf16[2,2,1024]{2,1,0:T(2,128)(2,1)S(1)}, bf16[2,2,1024]{2,1,0:T(2,128)(2,1)}, u32[]{:S(2)}) copy-start(bf16[2,2,1024]{2,1,0:T(2,128)(2,1)} %traces.1) | copy-start | bytes 24580
  1.4 0.7 %copy-start.2 = (s32[2,2]{1,0:T(2,128)S(1)}, s32[2,2]{1,0:T(2,128)}, u32[]{:S(2)}) copy-start(s32[2,2]{1,0:T(2,128)} %aperture.1) | copy-start | bytes 52
  2.0 0.8 %copy-start = (bf16[2,8,1024]{2,1,0:T(8,128)(2,1)S(1)}, bf16[2,8,1024]{2,1,0:T(8,128)(2,1)}, u32[]{:S(2)}) copy-start(bf16[2,8,1024]{2,1,0:T(8,128)(2,1)} %param.6) | copy-start | bytes 98308

commit v2 on v1

--- a/solution.py
+++ b/solution.py
@@ -45,9 +45,9 @@
     lane = lane_index(16)
 
     def one(g, carry):
-        base = g * 256 + s * 16
+        base = g * 32 + s * 16
         tiles = [
-            jnp.concatenate([wide[pl.ds(base + p * 8 + q, 8, stride=32), :] for p in range(2)], 0)
+            jnp.concatenate([wide[pl.ds(base + p * 8 + q, 8, stride=64), :] for p in range(2)], 0)
             for q in range(8)
         ]
         for m in range(8):
@@ -96,17 +96,17 @@
 
 def kernel(
     panels, traces, aperture, lo, hi, out,
-    trace_raw, aperture_raw, lo_raw, hi_raw, trace_wide, trace_out, window_out,
+    trace_raw, aperture_raw, lo_raw, hi_raw, windows, trace_wide, trace_out, window_out,
     panel_in, trace_in, window_in, wide, left, right, result_out,
     local_sem, panel_send, panel_recv, pass_send, pass_recv,
-    trace_send, trace_recv, window_send, window_recv, result_send, result_recv,
+    line_send, line_recv, trace_send, trace_recv, window_send, window_recv, result_send, result_recv,
 ):
     shot, point = lax.axis_index("shot"), lax.axis_index("point")
     y, zh = shot // 4, shot % 4
     zl, x, core = point // 8, (point // 2) % 4, point % 2
     z = zh * 2 + zl
     half = zh // 2
-    place = zl * 4 + x
+    place = x * 2 + zl
 
     def start(source, target, send, recv, to):
         pltpu.make_async_remote_copy(
@@ -116,6 +116,27 @@
     def landed(ref, sem):
         pltpu.make_async_copy(ref, ref, sem).wait()
 
+    barrier = pltpu.get_barrier_semaphore()
+
+    def greet(to):
+        pl.semaphore_signal(barrier, inc=1, device_id=to, device_id_type=MESH)
+
+    def greet_panels(i, carry):
+        greet(device(zl * 4 + x, zh, i // 4, i % 4, core))
+        return carry
+
+    def greet_line(i, carry):
+        greet(device(y, core * 2 + i // 4, (i // 2) % 2, x, i % 2))
+        return carry
+
+    lax.fori_loop(0, 8, greet_panels, 0)
+    lax.fori_loop(0, 8, greet_line, 0)
+    for i in range(2):
+        greet(device(y, core * 2 + i, zl, x, half))
+    for i in range(1, 4):
+        greet(device(y, zh, zl, (x + i) % 4, core))
+    greet(device(y, zh, zl, x, 1 - core))
+
     loads = [
         pltpu.make_async_copy(source, target, local_sem.at[i])
         for i, (source, target) in enumerate(
@@ -124,25 +145,6 @@
     ]
     for load in loads:
         load.start()
-
-    barrier = pltpu.get_barrier_semaphore()
-
-    def greet(to):
-        pl.semaphore_signal(barrier, inc=1, device_id=to, device_id_type=MESH)
-
-    def greet_traces(i, carry):
-        greet(device(y, core * 2 + i // 16, (i // 8) % 2, (i // 2) % 4, i % 2))
-        return carry
-
-    def greet_panels(i, carry):
-        greet(device(place, zh, i // 4, i % 4, core))
-        return carry
-
-    lax.fori_loop(0, 32, greet_traces, 0)
-    lax.fori_loop(0, 8, greet_panels, 0)
-    for i in range(2):
-        greet(device(y, core * 2 + i, zl, x, half))
-    greet(device(y, zh, zl, x, 1 - core))
 
     for load in loads:
         load.wait()
@@ -153,13 +155,15 @@
             for q in range(8):
                 trace_wide[s * 16 + p * 8 + q : s * 16 + p * 8 + q + 1, :] = kept[:, q * 128 : (q + 1) * 128]
     trace_out[...] = trace_wide[...].astype(BF16)
-    window_out[:, 0:2] = lo_raw[...].astype(F32)
-    window_out[:, 2:4] = hi_raw[...].astype(F32)
+    windows[...] = jnp.zeros_like(windows)
+    windows[0:2, 0:16] = lo_raw[...].astype(F32)
+    windows[2:4, 0:16] = hi_raw[...].astype(F32)
+    window_out[:, 0:8] = windows[...].T[:16]
     for slot in range(4):
         for g in range(2):
             right[slot, 1536 + g * 256 + 128 : 1536 + g * 256 + 256, 0:128] = jnp.zeros((128, 128), BF16)
 
-    pl.semaphore_wait(barrier, 43)
+    pl.semaphore_wait(barrier, 22)
 
     mine = (y // 4 == zl) & (y % 4 == x)
 
@@ -183,28 +187,24 @@
             panels, panel_in.at[0, place], panel_send, panel_recv.at[place], device(y, zh, y // 4, y % 4, core)
         )
 
-    trace_slot = (zh % 2) * 16 + ((core + half) % 2) * 8 + place
-    trace_sem = trace_recv.at[zh % 2]
-    trace_target = trace_in.at[trace_slot]
+    line_slot = (zh % 2) * 16 + place * 2 + (core + half) % 2
+    line_sem = line_recv.at[zh % 2 * 2 + zl]
+    line_target = trace_in.at[line_slot]
 
     def send_trace(i, carry):
-        o = i // 4
-        dz = 4 + ((o + 1) // 2) * (2 * ((o + 1) % 2) - 1)
-        to = (z + dz) % 8
-        start(
-            trace_out, trace_target, trace_send, trace_sem, device(y, to // 2, to % 2, (x + 3 - i % 4) % 4, half)
-        )
-        return carry
-
-    lax.fori_loop(0, 31, send_trace, 0)
+        to = (z + 4 + ((i + 1) // 2) * (2 * ((i + 1) % 2) - 1)) % 8
+        start(trace_out, line_target, line_send, line_sem, device(y, to // 2, to % 2, x, half))
+        return carry
+
+    lax.fori_loop(0, 7, send_trace, 0)
 
     @pl.when(core == half)
     def _():
-        pltpu.make_async_copy(trace_out, trace_target, trace_sem).start()
+        pltpu.make_async_copy(trace_out, line_target, line_sem).start()
 
     @pl.when(core != half)
     def _():
-        start(trace_out, trace_target, trace_send, trace_sem, device(y, zh, zl, x, half))
+        start(trace_out, line_target, line_send, line_sem, device(y, zh, zl, x, half))
 
     for i in range(2):
         rows = window_out.at[pl.ds(i * 8, 8)]
@@ -220,6 +220,14 @@
         def _():
             start(rows, target, window_send.at[i], sem, device(y, to, zl, x, half))
 
+    apart = 2 * ((half + core) % 2)
+    for i in range(4):
+        which = (z + (apart, 1, 3, 2 - apart)[i]) % 4
+        pair = trace_in.at[pl.ds(which // 2 * 16 + (x * 2 + which % 2) * 2, 2)]
+        landed(pair, line_recv.at[which])
+        for d in (2, 1, 3):
+            start(pair, pair, trace_send, trace_recv.at[which // 2], device(y, zh, zl, (x + d) % 4, core))
+
     for b in range(8):
         landed(panel_in.at[0, b], panel_recv.at[b])
         start(
@@ -227,7 +235,7 @@
         )
     spread_panels(panel_in, left, 0)
     for part in range(2):
-        landed(trace_in.at[pl.ds(part * 16, 16)], trace_recv.at[part])
+        landed(trace_in.at[pl.ds(part * 16, 12)], trace_recv.at[part])
         wide[...] = trace_in[part * 16 : part * 16 + 16].reshape(512, 128).astype(F32)
         for s in range(2):
             shift_traces(wide, right, part * 2 + s, s)
@@ -269,12 +277,13 @@
 
     @pl.when(core == half)
     def _():
-        landed(trace_in.at[pl.ds(0, 31)], trace_send)
+        landed(trace_in.at[pl.ds(0, 7)], line_send)
 
     @pl.when(core != half)
     def _():
-        landed(trace_in, trace_send)
-
+        landed(trace_in.at[pl.ds(0, 8)], line_send)
+
+    landed(trace_in.at[pl.ds(0, 24)], trace_send)
     landed(panel_in.at[1], pass_send)
     for i in range(2):
         same = (core == half) & (zh % 2 == i)
@@ -286,17 +295,18 @@
 
 
 def body(traces, panels, aperture, window_lo, window_hi):
-    anywhere = pl.BlockSpec(memory_space=pl.ANY)
+    anywhere = pl.BlockSpec(memory_space=pltpu.HBM)
     out = pl.pallas_call(
         kernel,
-        out_shape=jax.ShapeDtypeStruct((2, 16, 1024), BF16),
+        out_shape=pltpu.VMEM((2, 16, 1024), BF16),
         in_specs=[anywhere] * 5,
         out_specs=pl.BlockSpec(memory_space=pltpu.VMEM),
         scratch_shapes=[
             pltpu.VMEM((2, 2, 1024), BF16),
             pltpu.VMEM((2, 2), jnp.int32),
-            pltpu.VMEM((16, 2), jnp.int32),
-            pltpu.VMEM((16, 2), jnp.int32),
+            pltpu.VMEM((2, 16), jnp.int32),
+            pltpu.VMEM((2, 16), jnp.int32),
+            pltpu.VMEM((8, 128), F32),
             pltpu.VMEM((32, 128), F32),
             pltpu.VMEM((32, 128), BF16),
             pltpu.VMEM((16, 128), F32),
@@ -313,6 +323,8 @@
             pltpu.SemaphoreType.DMA,
             pltpu.SemaphoreType.DMA,
             pltpu.SemaphoreType.DMA,
+            pltpu.SemaphoreType.DMA((4,)),
+            pltpu.SemaphoreType.DMA,
             pltpu.SemaphoreType.DMA((2,)),
             pltpu.SemaphoreType.DMA((2,)),
             pltpu.SemaphoreType.DMA((2,)),
@@ -320,9 +332,9 @@
             pltpu.SemaphoreType.DMA((2,)),
         ],
         compiler_params=pltpu.CompilerParams(
-            collective_id=0, has_side_effects=True, vmem_limit_bytes=40 << 20
+            collective_id=0, has_side_effects=True, vmem_limit_bytes=60 << 20
         ),
-    )(panels.reshape(16, 1024), traces, aperture, window_lo, window_hi)
+    )(panels.reshape(16, 1024), traces, aperture, window_lo.T, window_hi.T)
     return out.reshape(2, 2, 8, 1024).transpose(0, 2, 1, 3).reshape(16, 2, 1024)
 
 

time: 37.5 us -> 33.7 us (0.90)
  the two profiles are of different devices: /device:TPU:1 before, /device:TPU:9 now
where the time goes in v2:
time: 33.7 us; the launch traced here: 33.5 us
  Pallas kernels  32.8 us (97%)
  local copies, waits for them, and re-layouts  0.7 us (2%)
    pallas_call x1, Pallas kernels, body(): pl.pallas_call(kernel, out_shape=pltpu.VMEM((2, 16, 1024), BF16), in_spec...  32.8 us
    transpose x1, local copies, waits for them, and re-layouts, body(): return out.reshape(2, 2, 8, 1024).transpose(0, 2, 1, 3).reshape(16, 2, 1024)  0.7 us

profile of v2, /device:TPU:9, one launch (start us, length us, event | category | flops | bytes accessed | tf_op | source)
XLA Modules:
  0.0 33.5 jit_solution(12678381213423510385)
XLA Ops:
  0.0 32.8 %shard_map.55 = bf16[2,16,1024]{2,1,0:T(8,128)(2,1)S(1)} custom-call(bf16[16,1024]{1,0:T(8,128)(2,1)} %bitcast.8, bf16[2,2,1024]{2,1,0:T(2,128)(2,1)} %traces.1, s32[2,2]{1,0:T(2,128)} %aperture.1, s32[2,16]{1,0:T(2,128)} %bitcast.9, s32[2,16]{1,0:T(2,128)} %bitcast.10), custom_call_target="tpu_custom_call" | custom-call | tf_op jit(solution)/shard_map/pallas_call | solution.py:299
  32.8 0.7 %copy.6 = bf16[2,8,2,1024]{3,2,1,0:T(2,128)(2,1)} copy(bf16[2,8,2,1024]{3,1,2,0:T(8,128)(2,1)S(1)} %bitcast.7) | data formatting | bytes 131072 | tf_op jit(solution)/shard_map/transpose | solution.py:338

commit v3 on v2

--- a/solution.py
+++ b/solution.py
@@ -44,7 +44,7 @@
 def shift_traces(wide, right, slot, s):
     lane = lane_index(16)
 
-    def one(g, carry):
+    for g in range(2):
         base = g * 32 + s * 16
         tiles = [
             jnp.concatenate([wide[pl.ds(base + p * 8 + q, 8, stride=64), :] for p in range(2)], 0)
@@ -60,11 +60,8 @@
                 for h in range(2):
                     k = q + h
                     if k < 8:
-                        row = pl.multiple_of((3 - k // 2) * 512 + g * 256 + h * 128 + m * 16, 16)
-                        right[slot, pl.ds(row, 16), (k % 2) * 128 : (k % 2) * 128 + 128] = value
-        return carry
-
-    lax.fori_loop(0, 2, one, 0)
+                        row = (3 - k // 2) * 512 + g * 256 + h * 128 + m * 16
+                        right[slot, row : row + 16, (k % 2) * 128 : (k % 2) * 128 + 128] = value
 
 
 def convolve(left, right, slot):
@@ -234,16 +231,14 @@
             panel_in.at[0, b], panel_in.at[1, b], pass_send, pass_recv, device(y, zh, zl, x, 1 - core)
         )
     spread_panels(panel_in, left, 0)
-    for part in range(2):
-        landed(trace_in.at[pl.ds(part * 16, 12)], trace_recv.at[part])
-        wide[...] = trace_in[part * 16 : part * 16 + 16].reshape(512, 128).astype(F32)
-        for s in range(2):
-            shift_traces(wide, right, part * 2 + s, s)
     landed(panel_in.at[1], pass_recv)
     spread_panels(panel_in, left, 1)
     for part in range(2):
         landed(window_in.at[part], window_recv.at[part])
+        landed(trace_in.at[pl.ds(part * 16, 12)], trace_recv.at[part])
+        wide[part] = trace_in[part * 16 : part * 16 + 16].reshape(512, 128).astype(F32)
         for s in range(2):
+            shift_traces(wide.at[part], right, part * 2 + s, s)
             value = weigh(
                 convolve(left, right, part * 2 + s),
                 window_in[part, :, s : s + 1],
@@ -313,7 +308,7 @@
             pltpu.VMEM((2, 8, 16, 1024), BF16),
             pltpu.VMEM((32, 32, 128), BF16),
             pltpu.VMEM((2, 8, 128), F32),
-            pltpu.VMEM((512, 128), F32),
+            pltpu.VMEM((2, 512, 128), F32),
             pltpu.VMEM((128, 2048), BF16),
             pltpu.VMEM((4, 2048, 256), BF16),
             pltpu.VMEM((2, 16, 1024), BF16),

time: 33.7 us -> 31.7 us (0.941)
  Pallas kernels: 32.8 us -> 30.9 us
    pallas_call x1, Pallas kernels: 32.8 us -> 30.9 us  [body(): pl.pallas_call(kernel, out_shape=pltpu.VMEM((2, 16, 1024), BF16), in_spec...]
where the time goes in v3:
time: 31.7 us; the launch traced here: 31.6 us
  Pallas kernels  30.9 us (97%)
  local copies, waits for them, and re-layouts  0.7 us (2%)
    pallas_call x1, Pallas kernels, body(): pl.pallas_call(kernel, out_shape=pltpu.VMEM((2, 16, 1024), BF16), in_spec...  30.9 us
    transpose x1, local copies, waits for them, and re-layouts, body(): return out.reshape(2, 2, 8, 1024).transpose(0, 2, 1, 3).reshape(16, 2, 1024)  0.7 us

profile of v3, /device:TPU:9, one launch (start us, length us, event | category | flops | bytes accessed | tf_op | source)
XLA Modules:
  0.0 31.6 jit_solution(3608204859098338354)
XLA Ops:
  0.0 30.9 %shard_map.55 = bf16[2,16,1024]{2,1,0:T(8,128)(2,1)S(1)} custom-call(bf16[16,1024]{1,0:T(8,128)(2,1)} %bitcast.8, bf16[2,2,1024]{2,1,0:T(2,128)(2,1)} %traces.1, s32[2,2]{1,0:T(2,128)} %aperture.1, s32[2,16]{1,0:T(2,128)} %bitcast.9, s32[2,16]{1,0:T(2,128)} %bitcast.10), custom_call_target="tpu_custom_call" | custom-call | tf_op jit(solution)/shard_map/pallas_call | solution.py:294
  30.9 0.7 %copy.6 = bf16[2,8,2,1024]{3,2,1,0:T(2,128)(2,1)} copy(bf16[2,8,2,1024]{3,1,2,0:T(8,128)(2,1)S(1)} %bitcast.7) | data formatting | bytes 131072 | tf_op jit(solution)/shard_map/transpose | solution.py:333

commit v4 on v3

--- a/solution.py
+++ b/solution.py
@@ -19,26 +19,30 @@
 
 def spread_panels(panel_in, left, g):
     for first in (0, 4):
-        blocks = [
-            [panel_in[g, b, :, q * 128 : (q + 1) * 128].astype(F32) for b in range(8)]
-            for q in range(first, first + 4)
+        rows = [
+            jnp.concatenate([panel_in[g, b, :, q * 128 : (q + 1) * 128] for q in range(first, first + 4)], 0)
+            for b in range(8)
         ]
-        rows = [jnp.concatenate([b[p][:8] for b in blocks], 0) for p in range(8)]
-        rows += [jnp.concatenate([b[p][8:] for b in blocks], 0) for p in range(8)]
-        lane = lane_index(32)
-        for bit in (1, 2, 4, 8):
+        lane = lane_index(64)
+        for bit in (1, 2, 4):
             low = (lane & bit) == 0
             new = list(rows)
-            for p in range(16):
+            for p in range(8):
                 if not p & bit:
                     lo, hi = rows[p], rows[p | bit]
                     new[p] = jnp.where(low, lo, pltpu.roll(hi, bit, 1))
                     new[p | bit] = jnp.where(low, pltpu.roll(lo, 128 - bit, 1), hi)
             rows = new
+        low = (lane_index(8) & 8) == 0
         for i in range(4):
             q = first + i
+            lower, upper = [], []
+            for v in rows:
+                v = v[16 * i : 16 * i + 16].astype(F32)
+                lower.append(jnp.where(low, v[:8], pltpu.roll(v[8:], 8, 1)))
+                upper.append(jnp.where(low, pltpu.roll(v[:8], 120, 1), v[8:]))
             at = ((q // 2) * 4 + g * 2 + q % 2) * 128
-            left[:, at : at + 128] = jnp.concatenate([v[8 * i : 8 * i + 8] for v in rows], 0).astype(BF16)
+            left[:, at : at + 128] = jnp.concatenate(lower + upper, 0).astype(BF16)
 
 
 def shift_traces(wide, right, slot, s):

time: 31.7 us -> 31.8 us (level)
  no operation moved by 1% of the time
where the time goes in v4:
time: 31.8 us; the launch traced here: 31.6 us
  Pallas kernels  30.9 us (97%)
  local copies, waits for them, and re-layouts  0.7 us (2%)
    pallas_call x1, Pallas kernels, body(): pl.pallas_call(kernel, out_shape=pltpu.VMEM((2, 16, 1024), BF16), in_spec...  30.9 us
    transpose x1, local copies, waits for them, and re-layouts, body(): return out.reshape(2, 2, 8, 1024).transpose(0, 2, 1, 3).reshape(16, 2, 1024)  0.7 us

profile of v4, /device:TPU:9, one launch (start us, length us, event | category | flops | bytes accessed | tf_op | source)
XLA Modules:
  0.0 31.6 jit_solution(4694939370675377979)
XLA Ops:
  0.0 30.9 %shard_map.55 = bf16[2,16,1024]{2,1,0:T(8,128)(2,1)S(1)} custom-call(bf16[16,1024]{1,0:T(8,128)(2,1)} %bitcast.8, bf16[2,2,1024]{2,1,0:T(2,128)(2,1)} %traces.1, s32[2,2]{1,0:T(2,128)} %aperture.1, s32[2,16]{1,0:T(2,128)} %bitcast.9, s32[2,16]{1,0:T(2,128)} %bitcast.10), custom_call_target="tpu_custom_call" | custom-call | tf_op jit(solution)/shard_map/pallas_call | solution.py:298
  30.9 0.7 %copy.6 = bf16[2,8,2,1024]{3,2,1,0:T(2,128)(2,1)} copy(bf16[2,8,2,1024]{3,1,2,0:T(8,128)(2,1)S(1)} %bitcast.7) | data formatting | bytes 131072 | tf_op jit(solution)/shard_map/transpose | solution.py:337
